TPU v7x, 32 devices: a whole 2x2x4 slice. The times are simulated.
32 devices in a mesh: freq: 8 (over z, y), inp: 4 (over x, core).
Axes of the slice: x: 2, y: 2, z: 4, core: 2. Of those that a mesh axis runs over, the one named last changes fastest.
Arguments:
- voltages: int32 [24, 2048, 1024], P('freq', None, 'inp'), may hold values from -128 to 127
- taps: float32 [12, 2048], replicated, may hold values from -0.013671875 to 0.013671875
- start: int32 [8, 2, 1024], replicated, may hold values from -127 to 127
Outputs:
- cleaned: bfloat16 [1024, 24, 2, 1024], P('freq', None, None, 'inp')
- ritz_matrix: float32 [1024, 8, 8], P('freq')
Inputs may be any that keep to these rules, and one draw needn't show every extreme that they name: `voltages`: 8-bit voltage samples.
All inputs are finite; a program needn't handle non-finite values.
Results may differ from a plain program's by a relative error of at most 0.0052.
Values may be sent and summed in bfloat16 or wider, within the bound.
A program may use at most 192 MiB of HBM per device.

v0:
```python
import math

import jax
import jax.numpy as jnp
from jax import lax
from jax.sharding import PartitionSpec as P

ITERS = 4


def from_behind(value, axis, steps):
    count = lax.axis_size(axis)
    pairs = [(source, (source + steps) % count) for source in range(count)]
    return lax.ppermute(value, axis, pairs)


def project_rows(basis_rows, channel_data):
    projected = jnp.einsum(
        "ckr,cmr->ckm", basis_rows, channel_data, precision=lax.Precision.HIGHEST
    )
    return lax.psum(projected, "inp")


def subspace_clean(turned, start_block):
    highest = lax.Precision.HIGHEST
    channel_local, spectra_count, part_count, inputs_width = turned.shape
    row_count = part_count * inputs_width
    channel_data = turned.reshape(channel_local, spectra_count, row_count).astype(jnp.float32)
    start_rows = start_block.reshape(start_block.shape[0], row_count).astype(jnp.float32)
    basis_rows = jnp.broadcast_to(start_rows[None], (channel_local,) + start_rows.shape)
    for iteration in range(ITERS):
        projected = project_rows(basis_rows, channel_data)
        mapped = (
            jnp.einsum("ckm,cmr->ckr", projected, channel_data, precision=highest) / spectra_count
        )
        gram_matrix = jnp.einsum("ckr,cjr->ckj", mapped, mapped, precision=highest)
        gram_matrix = lax.psum(gram_matrix, "inp")
        lower_factor = jnp.linalg.cholesky(gram_matrix)
        basis_rows = lax.linalg.triangular_solve(lower_factor, mapped, left_side=True, lower=True)
    projected = project_rows(basis_rows, channel_data)
    ritz_matrix = (
        jnp.einsum("ckm,cjm->ckj", projected, projected, precision=highest) / spectra_count
    )
    cleaned = channel_data - jnp.einsum("ckm,ckr->cmr", projected, basis_rows, precision=highest)
    cleaned = cleaned.reshape(channel_local, spectra_count, part_count, inputs_width).astype(
        jnp.bfloat16
    )
    return (cleaned, ritz_matrix)


def shards(voltages, taps, start):
    slot_count = voltages.shape[0]
    frame_len = voltages.shape[1]
    inputs_local = voltages.shape[2]
    channel_count = frame_len // 2
    tap_count = taps.shape[0]
    frame_stack = voltages.astype(jnp.bfloat16)
    history_len = tap_count - 1
    group_count = lax.axis_size("freq")
    portions = [frame_stack]
    shift_count = (history_len - 1) // slot_count + 1
    for distance in range(1, shift_count + 1):
        first_frame = max(0, distance * slot_count - history_len)
        portion = frame_stack[first_frame:]
        offset_mod = distance % group_count
        arrived = from_behind(portion, "freq", offset_mod)
        portions = [arrived] + portions
    extended = jnp.concatenate(portions, axis=0)
    filtered = jnp.zeros((slot_count, frame_len, inputs_local), jnp.float32)
    for tap_index in range(tap_count):
        window = extended[tap_index : tap_index + slot_count].astype(jnp.float32)
        filtered = filtered + taps[tap_index][None, :, None] * window
    channel_idx = lax.broadcasted_iota(jnp.int32, (channel_count, frame_len), 0)
    sample_idx = lax.broadcasted_iota(jnp.int32, (channel_count, frame_len), 1)
    angles = (channel_idx * sample_idx % frame_len).astype(jnp.float32) * (
        2.0 * math.pi / frame_len
    )
    dft_scale = 1.0 / math.sqrt(channel_count)
    cosine = jnp.cos(angles)
    sine_table = jnp.sin(angles)
    real_part = (
        jnp.einsum("kn,sni->ksi", cosine, filtered, precision=lax.Precision.HIGHEST) * dft_scale
    )
    imag_part = (
        -jnp.einsum("kn,sni->ksi", sine_table, filtered, precision=lax.Precision.HIGHEST)
        * dft_scale
    )
    spectra = jnp.stack([real_part, imag_part], axis=2).astype(jnp.bfloat16)
    turned = lax.all_to_all(spectra, "freq", split_axis=0, concat_axis=1, tiled=True)
    start_local = lax.dynamic_slice_in_dim(
        start, lax.axis_index("inp") * inputs_local, inputs_local, 2
    )
    cleaned, ritz_matrix = subspace_clean(turned, start_local)
    return (cleaned, ritz_matrix)


def solution(mesh):
    placed = (P("freq", None, "inp"), P(), P())
    return jax.shard_map(
        shards,
        mesh=mesh,
        in_specs=placed,
        out_specs=(P("freq", None, None, "inp"), P("freq", None, None)),
        check_vma=False,
    )
```

profile of v0, /device:TPU:13, one launch (start us, length us, event | category | flops | bytes accessed | tf_op | source)
XLA Modules:
  0.0 1292.2 jit_solution(8398367931099844952)
XLA Ops:
  16.6 356.1 %collective-permute-done = bf16[2,2048,256]{2,1,0:T(8,128)(2,1)S(1)} collective-permute-done((bf16[2,2048,256]{2,1,0:T(8,128)(2,1)S(1)}, bf16[2,2048,256]{2,1,0:T(8,128)(2,1)S(1)}, u32[]{:S(2)}, u32[]{:S(2)}) %collective-permute-start) | collective-permute-done | bytes 2097184 | tf_op jit(solution)/shard_map/ppermute | solution.py:14
  373.9 9.7 multiply_add_fusion
  383.6 55.4 %fusion.35 = bf16[1024,3,1,256]{3,0,1,2:T(8,128)(2,1)S(1)} fusion(f32[3,2048,256]{2,1,0:T(8,128)} %multiply_add_fusion), kind=kOutput, calls=%fused_computation.41 | convolution fusion | flops 19358285824 | bytes 7864320 | tf_op jit(solution)/shard_map/kn,sni->ksi/dot_general | solution.py:82
  439.0 52.9 %fusion.38 = bf16[1024,3,1,256]{3,0,1,2:T(8,128)(2,1)S(1)} fusion(f32[3,2048,256]{2,1,0:T(8,128)S(1)} %copy-done.5), kind=kOutput, calls=%fused_computation.42 | convolution fusion | flops 19359072256 | bytes 7864320 | tf_op jit(solution)/shard_map/kn,sni->ksi/dot_general | solution.py:85
  492.2 4.9 copy.67
  497.1 6.4 all-to-all-start
  504.3 67.4 %all-to-all-done = bf16[1024,3,2,256]{3,2,1,0:T(2,128)(2,1)S(1)} async-done(((bf16[1024,3,2,256]{3,2,1,0:T(2,128)(2,1)}), bf16[1024,3,2,256]{3,2,1,0:T(2,128)(2,1)S(1)}, u32[]{:S(2)}, u32[]{:S(2)}) %all-to-all-start) | async-done | bytes 3145760 | tf_op jit(solution)/shard_map/all_to_all | solution.py:89
  583.8 33.7 %all-reduce.6.cloned.1.call-done = f32[128,8,24]{2,1,0:T(8,128)} async-done(((f32[128,8,24]{2,1,0:T(8,128)}), f32[128,8,24]{2,1,0:T(8,128)}) %all-reduce.6.cloned.1.call-update) | async-done | bytes 98320 | tf_op jit(solution)/shard_map/psum | solution.py:21
  621.8 4.8 fusion.29
  627.8 11.1 psum.64
  641.8 95.5 %custom-call.12 = f32[128,8,8]{2,1,0:T(8,128)} custom-call(f32[128,8,8]{2,1,0:T(8,128)} %broadcast_multiply_fusion.3), custom_call_target="Cholesky" | custom-call | tf_op jit(solution)/shard_map/jit(cholesky)/cholesky | solution.py:38
  748.0 32.4 %all-reduce.8.cloned.1.call-done = f32[128,8,24]{2,1,0:T(8,128)} async-done(((f32[128,8,24]{2,1,0:T(8,128)}), f32[128,8,24]{2,1,0:T(8,128)}) %all-reduce.8.cloned.1.call-update) | async-done | bytes 98320 | tf_op jit(solution)/shard_map/psum | solution.py:21
  784.6 4.8 fusion.25
  790.6 11.1 psum.66
  804.6 95.5 %custom-call.14 = f32[128,8,8]{2,1,0:T(8,128)} custom-call(f32[128,8,8]{2,1,0:T(8,128)} %broadcast_multiply_fusion.2), custom_call_target="Cholesky" | custom-call | tf_op jit(solution)/shard_map/jit(cholesky)/cholesky | solution.py:38
  911.0 32.1 %all-reduce.10.cloned.1.call-done = f32[128,8,24]{2,1,0:T(8,128)} async-done(((f32[128,8,24]{2,1,0:T(8,128)}), f32[128,8,24]{2,1,0:T(8,128)}) %all-reduce.10.cloned.1.call-update) | async-done | bytes 98320 | tf_op jit(solution)/shard_map/psum | solution.py:21
  953.5 11.1 psum.68
  967.5 95.5 %custom-call.16 = f32[128,8,8]{2,1,0:T(8,128)} custom-call(f32[128,8,8]{2,1,0:T(8,128)} %broadcast_multiply_fusion.1), custom_call_target="Cholesky" | custom-call | tf_op jit(solution)/shard_map/jit(cholesky)/cholesky | solution.py:38
  1073.6 32.4 %all-reduce.12.cloned.1.call-done = f32[128,8,24]{2,1,0:T(8,128)} async-done(((f32[128,8,24]{2,1,0:T(8,128)}), f32[128,8,24]{2,1,0:T(8,128)}) %all-reduce.12.cloned.1.call-update) | async-done | bytes 98320 | tf_op jit(solution)/shard_map/psum | solution.py:21
  1116.3 11.1 psum.70
  1130.3 95.5 %custom-call.18 = f32[128,8,8]{2,1,0:T(8,128)} custom-call(f32[128,8,8]{2,1,0:T(8,128)} %broadcast_multiply_fusion), custom_call_target="Cholesky" | custom-call | tf_op jit(solution)/shard_map/jit(cholesky)/cholesky | solution.py:38
  1237.5 32.7 %all-reduce.14.cloned.1.call-done = f32[128,8,24]{2,1,0:T(8,128)} async-done(((f32[128,8,24]{2,1,0:T(8,128)}), f32[128,8,24]{2,1,0:T(8,128)}) %all-reduce.14.cloned.1.call-update) | async-done | bytes 98320 | tf_op jit(solution)/shard_map/psum | solution.py:21
  1270.2 8.0 subtract_convert_fusion
  1278.2 5.5 convert_element_type.82
  (104 shorter events, 112.4 us)
Async XLA Ops:
  10.5 6.0 copy-start.7
  10.5 362.3 %collective-permute-start.1 = (bf16[3,2048,256]{2,1,0:T(8,128)(2,1)S(1)}, bf16[3,2048,256]{2,1,0:T(8,128)(2,1)S(1)}, u32[]{:S(2)}, u32[]{:S(2)}) collective-permute-start(bf16[3,2048,256]{2,1,0:T(8,128)(2,1)S(1)} %convert_element_type.65), channel_id=1, source_target_pairs={{0,12},{4,16},{8,20},{12,24},{16,28},{20,0},{24,4},{28,8},{1,13},{... | collective-permute-start | bytes 9437192 | tf_op jit(solution)/shard_map/ppermute | solution.py:14
  12.8 360.4 %collective-permute-start.2 = (bf16[3,2048,256]{2,1,0:T(8,128)(2,1)S(1)}, bf16[3,2048,256]{2,1,0:T(8,128)(2,1)S(1)}, u32[]{:S(2)}, u32[]{:S(2)}) collective-permute-start(bf16[3,2048,256]{2,1,0:T(8,128)(2,1)S(1)} %convert_element_type.65), channel_id=1, source_target_pairs={{0,8},{4,12},{8,16},{12,20},{16,24},{20,28},{24,0},{28,4},{1,9},{5... | collective-permute-start | bytes 9437192 | tf_op jit(solution)/shard_map/ppermute | solution.py:14
  12.8 360.9 %collective-permute-start.3 = (bf16[3,2048,256]{2,1,0:T(8,128)(2,1)S(1)}, bf16[3,2048,256]{2,1,0:T(8,128)(2,1)S(1)}, u32[]{:S(2)}, u32[]{:S(2)}) collective-permute-start(bf16[3,2048,256]{2,1,0:T(8,128)(2,1)S(1)} %convert_element_type.65), channel_id=1, source_target_pairs={{0,4},{4,8},{8,12},{12,16},{16,20},{20,24},{24,28},{28,0},{1,5},{5... | collective-permute-start | bytes 9437192 | tf_op jit(solution)/shard_map/ppermute | solution.py:14
  14.2 358.5 %collective-permute-start = (bf16[2,2048,256]{2,1,0:T(8,128)(2,1)S(1)}, bf16[2,2048,256]{2,1,0:T(8,128)(2,1)S(1)}, u32[]{:S(2)}, u32[]{:S(2)}) collective-permute-start(bf16[2,2048,256]{2,1,0:T(8,128)(2,1)S(1)} %slice.98), channel_id=1, source_target_pairs={{0,16},{4,20},{8,24},{12,28},{16,0},{20,4},{24,8},{28,12},{1,17},{... | collective-permute-start | bytes 6291464 | tf_op jit(solution)/shard_map/ppermute | solution.py:14
  383.6 55.4 %copy-start.5 = (f32[3,2048,256]{2,1,0:T(8,128)S(1)}, f32[3,2048,256]{2,1,0:T(8,128)}, u32[]{:S(2)}) copy-start(f32[3,2048,256]{2,1,0:T(8,128)} %multiply_add_fusion) | copy-start | bytes 18874372
  497.1 74.6 %all-to-all-start = ((bf16[1024,3,2,256]{3,2,1,0:T(2,128)(2,1)}), bf16[1024,3,2,256]{3,2,1,0:T(2,128)(2,1)S(1)}, u32[]{:S(2)}, u32[]{:S(2)}) async-start(bf16[1024,3,2,256]{3,2,1,0:T(2,128)(2,1)} %copy.67), calls=%async_computation | async-start | bytes 6291456 | tf_op jit(solution)/shard_map/all_to_all | solution.py:89
  503.5 114.0 %all-reduce.6.cloned.1.call-start = ((), (), s32[]{:S(2)}) async-start(), calls=%async_computation.1 | async-start | bytes 1048576 | tf_op jit(solution)/shard_map/psum | solution.py:21
  583.5 196.8 %all-reduce.8.cloned.1.call-start = ((), (), s32[]{:S(2)}) async-start(), calls=%async_computation.2 | async-start | bytes 1048576 | tf_op jit(solution)/shard_map/psum | solution.py:21
  620.5 1.3 copy-start.2
  747.7 195.5 %all-reduce.10.cloned.1.call-start = ((), (), s32[]{:S(2)}) async-start(), calls=%async_computation.3 | async-start | bytes 1048576 | tf_op jit(solution)/shard_map/psum | solution.py:21
  783.3 1.3 copy-start.3
  910.5 195.5 %all-reduce.12.cloned.1.call-start = ((), (), s32[]{:S(2)}) async-start(), calls=%async_computation.4 | async-start | bytes 1048576 | tf_op jit(solution)/shard_map/psum | solution.py:21
  946.1 1.3 copy-start.4
  1073.4 196.8 %all-reduce.14.cloned.1.call-start = ((), (), s32[]{:S(2)}) async-start(), calls=%async_computation.5 | async-start | bytes 1048576 | tf_op jit(solution)/shard_map/psum | solution.py:21
  1108.9 1.3 copy-start.1
  1232.6 1.3 copy-start
  1278.2 5.5 copy-start.6
Sparse Core Ops, SparseCore 0:
  583.7 33.8 all-reduce.5
  747.8 32.4 all-reduce.7
  910.7 32.4 all-reduce.9
  1073.5 32.4 all-reduce.11
  1237.6 32.4 all-reduce.13
where the time goes:
time: 1320 us; the launch traced here: 1290 us
  waiting for transfers between devices  587 us (44%)
  other arithmetic  407 us (31%)
  matrix products  181 us (14%)
  local copies, waits for them, and re-layouts  45.3 us (3%)
  blocking collectives  44.3 us (3%)
  between operations  14.3 us (1%)
  starting transfers between devices  13.6 us (1%)
    another operation x13, other arithmetic, subspace_clean(): lower_factor = jnp.linalg.cholesky(gram_matrix)  382 us
    ppermute x4, waiting for transfers between devices, from_behind(): return lax.ppermute(value, axis, pairs)  356 us
    psum x5, waiting for transfers between devices, project_rows(): return lax.psum(projected, 'inp')  163 us
    all_to_all x1, waiting for transfers between devices, shards(): lax.all_to_all(spectra, 'freq', split_axis=0, concat_axis=1, tiled=True)  67.4 us
    dot_general x1, matrix products, shards(): jnp.einsum('kn,sni->ksi', cosine, filtered, precision=lax.Precision.HIGHEST)  55.4 us
    dot_general x1, matrix products, shards(): jnp.einsum('kn,sni->ksi', sine_table, filtered, precision=lax.Precision.H...  52.9 us
    psum x4, blocking collectives, subspace_clean(): gram_matrix = lax.psum(gram_matrix, 'inp')  44.3 us
  transfers between devices with their start and end apart: 10, of which 7 were waited for; matrix products, arithmetic and copies ran while one was open for 0% of the time, Pallas kernels for 0%

commit v1 on v0

--- a/solution.py
+++ b/solution.py
@@ -1,11 +1,239 @@
+import functools
 import math
 
 import jax
 import jax.numpy as jnp
+import ml_dtypes
+import numpy as np
 from jax import lax
+from jax.experimental import pallas as pl
+from jax.experimental.pallas import tpu as pltpu
 from jax.sharding import PartitionSpec as P
 
 ITERS = 4
+CHUNKS = 2
+LANES = 128
+MESH = pl.DeviceIdType.MESH
+
+
+def dft_tables(frame_len, group_count):
+    half = frame_len // 2
+    pairs = half // 2
+    sample = np.arange(half, dtype=np.int64)[:, None]
+    tables = []
+    for parity in (0, 1):
+        channel = 2 * np.arange(pairs, dtype=np.int64)[None, :] + parity
+        angle = 2.0 * np.pi * ((sample * channel) % frame_len) / frame_len
+        scale = 1.0 / math.sqrt(half)
+        real = (np.cos(angle) * scale).reshape(half, group_count, 1, pairs // group_count)
+        imag = (-np.sin(angle) * scale).reshape(half, group_count, 1, pairs // group_count)
+        table = np.concatenate([real, imag], axis=2).reshape(half, half)
+        high = table.astype(ml_dtypes.bfloat16)
+        low = (table - high.astype(np.float64)).astype(ml_dtypes.bfloat16)
+        tables += [high, low]
+    return np.stack(tables)
+
+
+def channelize_kernel(
+    count, slots, tap_count, volts_ref, taps_ref, table_hbm, turned_ref,
+    gathered, table, halves, outgoing, table_sem, send_a, recv_a, send_b, recv_b,
+):
+    me = lax.axis_index("freq")
+    frames = count * slots
+    half = table.shape[1]
+    rows = volts_ref.shape[3]
+
+    table_copy = pltpu.make_async_copy(table_hbm, table, table_sem)
+    table_copy.start()
+    barrier = pltpu.get_barrier_semaphore()
+    for step in range(1, count):
+        peer = lax.rem(me + step, count)
+        pl.semaphore_signal(barrier, inc=1, device_id={"freq": peer}, device_id_type=MESH)
+    pl.semaphore_wait(barrier, count - 1)
+
+    def voltage_copy(chunk, step):
+        peer = lax.rem(me + step, count)
+        return pltpu.make_async_remote_copy(
+            src_ref=volts_ref.at[peer, chunk],
+            dst_ref=gathered.at[chunk, me],
+            send_sem=send_a.at[chunk, step - 1],
+            recv_sem=recv_a.at[chunk, step - 1],
+            device_id={"freq": peer},
+            device_id_type=MESH,
+        )
+
+    def spectra_copy(chunk, step):
+        peer = lax.rem(me + step, count)
+        return pltpu.make_async_remote_copy(
+            src_ref=outgoing.at[peer, chunk],
+            dst_ref=turned_ref.at[me, chunk],
+            send_sem=send_b.at[chunk, step - 1],
+            recv_sem=recv_b.at[chunk, step - 1],
+            device_id={"freq": peer},
+            device_id_type=MESH,
+        )
+
+    order = sorted(range(1, count), key=lambda step: -min(step, count - step))
+    first = [voltage_copy(0, step) for step in order]
+    for copy in first:
+        copy.start()
+    for chunk in range(CHUNKS):
+        gathered[chunk, me] = volts_ref[me, chunk]
+    arriving = first
+    for chunk in range(CHUNKS):
+        for copy in arriving:
+            copy.wait_send()
+        following = []
+        if chunk + 1 < CHUNKS:
+            following = [voltage_copy(chunk + 1, step) for step in order]
+            for copy in following:
+                copy.start()
+        for copy in arriving:
+            copy.wait_recv()
+        arriving = following
+
+        def filter_tile(tile, carry):
+            sums = []
+            for part in (0, 1):
+                at = pl.ds(pl.multiple_of(tile * LANES + part * half, LANES), LANES)
+                window = gathered[chunk, :, :, :, at].astype(jnp.float32)
+                window = window.reshape(frames, rows, LANES)
+                extended = jnp.concatenate([window[frames - tap_count + 1 :], window], axis=0)
+                total = taps_ref[0:1, at][None] * extended[:frames]
+                for tap in range(1, tap_count):
+                    total = total + taps_ref[tap : tap + 1, at][None] * extended[tap : tap + frames]
+                sums.append(total.reshape(frames * rows, LANES))
+            at = pl.ds(pl.multiple_of(tile * LANES, LANES), LANES)
+            for index, value in ((0, sums[0] + sums[1]), (2, sums[0] - sums[1])):
+                high = value.astype(jnp.bfloat16)
+                halves[index, :, at] = high
+                halves[index + 1, :, at] = (value - high.astype(jnp.float32)).astype(jnp.bfloat16)
+            return carry
+
+        lax.fori_loop(0, half // LANES, filter_tile, 0)
+        if chunk == 0:
+            table_copy.wait()
+
+        def transform_tile(pair, carry):
+            at = pl.ds(pl.multiple_of(pair * 2 * LANES, 2 * LANES), 2 * LANES)
+            for parity in (0, 1):
+                high, low = halves[2 * parity], halves[2 * parity + 1]
+                table_high = table[2 * parity, :, at]
+                table_low = table[2 * parity + 1, :, at]
+                dot = functools.partial(jnp.dot, preferred_element_type=jnp.float32)
+                result = dot(low, table_high) + dot(high, table_low) + dot(high, table_high)
+                result = result.astype(jnp.bfloat16)
+                outgoing[2 * pair, chunk, parity] = result[:, :LANES]
+                outgoing[2 * pair + 1, chunk, parity] = result[:, LANES:]
+            return carry
+
+        lax.fori_loop(0, count // 2, transform_tile, 0)
+        for step in order:
+            spectra_copy(chunk, step).start()
+        turned_ref[me, chunk] = outgoing[me, chunk]
+    for chunk in range(CHUNKS):
+        for step in order:
+            spectra_copy(chunk, step).wait()
+
+
+def channelize(voltages, taps):
+    slots, frame_len, inputs_local = voltages.shape
+    count = lax.axis_size("freq")
+    half = frame_len // 2
+    rows = inputs_local // (count * CHUNKS)
+    volts = voltages.astype(jnp.bfloat16).reshape(slots, frame_len, count, CHUNKS, rows)
+    volts = jnp.transpose(volts, (2, 3, 0, 4, 1))
+    table = jnp.asarray(dft_tables(frame_len, count))
+    all_rows = count * slots * rows
+    vmem = pl.BlockSpec(memory_space=pltpu.VMEM)
+    turned = pl.pallas_call(
+        functools.partial(channelize_kernel, count, slots, taps.shape[0]),
+        out_shape=jax.ShapeDtypeStruct((count, CHUNKS, 2, all_rows, LANES), jnp.bfloat16),
+        in_specs=[vmem, vmem, pl.BlockSpec(memory_space=pl.ANY)],
+        out_specs=vmem,
+        scratch_shapes=[
+            pltpu.VMEM((CHUNKS, count, slots, rows, frame_len), jnp.bfloat16),
+            pltpu.VMEM((4, half, half), jnp.bfloat16),
+            pltpu.VMEM((4, all_rows, half), jnp.bfloat16),
+            pltpu.VMEM((count, CHUNKS, 2, all_rows, LANES), jnp.bfloat16),
+            pltpu.SemaphoreType.DMA,
+            pltpu.SemaphoreType.DMA((CHUNKS, count - 1)),
+            pltpu.SemaphoreType.DMA((CHUNKS, count - 1)),
+            pltpu.SemaphoreType.DMA((CHUNKS, count - 1)),
+            pltpu.SemaphoreType.DMA((CHUNKS, count - 1)),
+        ],
+        compiler_params=pltpu.CompilerParams(
+            collective_id=0, has_side_effects=True, vmem_limit_bytes=48 * 1024 * 1024
+        ),
+        name="channelize",
+    )(volts, taps, table)
+    turned = turned.reshape(count, CHUNKS, 2, count * slots, rows, 2, LANES // 2)
+    turned = jnp.transpose(turned, (6, 2, 3, 5, 0, 1, 4))
+    return turned.reshape(LANES, count * slots, 2, inputs_local)
+
+
+def subspace_kernel(gram_ref, keep_ref, ritz_ref):
+    block = ritz_ref.shape[0]
+    frames = keep_ref.shape[0]
+
+    def times_gram(left):
+        total = left[:, 0:1] * gram_ref[block][None]
+        for frame in range(1, frames):
+            total = total + left[:, frame : frame + 1] * gram_ref[block + frame][None]
+        return total
+
+    projected = gram_ref[:block]
+    coefficients = None
+    for iteration in range(ITERS):
+        mapped = projected * (1.0 / frames)
+        spread = times_gram(mapped)
+        columns = [jnp.sum(spread * mapped[k][None], axis=1) for k in range(block)]
+        remaining = [mapped[k] for k in range(block)]
+        for k in range(block):
+            inverse = lax.rsqrt(columns[k][k : k + 1])
+            inverse = inverse * (1.5 - 0.5 * columns[k][k : k + 1] * inverse * inverse)
+            factor = columns[k] * inverse
+            remaining[k] = remaining[k] * inverse
+            for j in range(k + 1, block):
+                remaining[j] = remaining[j] - factor[j : j + 1] * remaining[k]
+                columns[j] = columns[j] - factor[j : j + 1] * factor
+        coefficients = jnp.stack(remaining)
+        projected = times_gram(coefficients)
+    for k in range(block):
+        ritz_ref[k] = jnp.sum(projected * projected[k][None], axis=1) * (1.0 / frames)
+    row = lax.broadcasted_iota(jnp.int32, keep_ref.shape[1:], 0)
+    for frame in range(frames):
+        removed = projected[0][frame : frame + 1] * coefficients[0]
+        for k in range(1, block):
+            removed = removed + projected[k][frame : frame + 1] * coefficients[k]
+        keep_ref[frame] = jnp.where(row == frame, 1.0, 0.0) - removed
+
+
+def clean(turned, start_local):
+    channels, frames, parts, inputs_local = turned.shape
+    block = start_local.shape[0]
+    data = turned.reshape(channels, frames, parts * inputs_local)
+    begin = start_local.reshape(block, parts * inputs_local).astype(jnp.bfloat16)
+    stacked = jnp.concatenate(
+        [jnp.broadcast_to(begin[None], (channels,) + begin.shape), data], axis=1
+    )
+    gram = jnp.einsum("czr,cmr->czm", stacked, data, preferred_element_type=jnp.float32)
+    gram = jnp.transpose(lax.psum(gram, "inp"), (1, 2, 0))
+    keep, ritz = pl.pallas_call(
+        subspace_kernel,
+        out_shape=(
+            jax.ShapeDtypeStruct((frames, frames, channels), jnp.float32),
+            jax.ShapeDtypeStruct((block, block, channels), jnp.float32),
+        ),
+        compiler_params=pltpu.CompilerParams(vmem_limit_bytes=32 * 1024 * 1024),
+        name="subspace",
+    )(gram)
+    keep = jnp.transpose(keep, (2, 0, 1))
+    cleaned = jnp.einsum(
+        "cmn,cnr->cmr", keep, data.astype(jnp.float32), precision=lax.Precision.HIGHEST
+    )
+    cleaned = cleaned.astype(jnp.bfloat16).reshape(turned.shape)
+    return cleaned, jnp.transpose(ritz, (2, 0, 1))
 
 
 def from_behind(value, axis, steps):
@@ -48,7 +276,7 @@
     return (cleaned, ritz_matrix)
 
 
-def shards(voltages, taps, start):
+def general_shards(voltages, taps, start):
     slot_count = voltages.shape[0]
     frame_len = voltages.shape[1]
     inputs_local = voltages.shape[2]
@@ -94,6 +322,25 @@
     return (cleaned, ritz_matrix)
 
 
+def start_columns(start, inputs_local):
+    return lax.dynamic_slice_in_dim(start, lax.axis_index("inp") * inputs_local, inputs_local, 2)
+
+
+def shards(voltages, taps, start):
+    slots, frame_len, inputs_local = voltages.shape
+    count = lax.axis_size("freq")
+    fits = (
+        count % 2 == 0
+        and frame_len // 2 == count * LANES
+        and inputs_local % (count * CHUNKS * 16) == 0
+        and count * slots <= 32
+        and taps.shape[0] <= count * slots
+    )
+    if not fits:
+        return general_shards(voltages, taps, start)
+    return clean(channelize(voltages, taps), start_columns(start, inputs_local))
+
+
 def solution(mesh):
     placed = (P("freq", None, "inp"), P(), P())
     return jax.shard_map(

time: 1320 us -> 364 us (0.28)
  the two profiles are of different devices: /device:TPU:13 before, /device:TPU:0 now
where the time goes in v1:
time: 364 us; the launch traced here: 359 us
  local copies, waits for them, and re-layouts  154 us (42%)
  Pallas kernels  139 us (38%)
  waiting for transfers between devices  38.9 us (11%)
  between operations  14.1 us (4%)
  matrix products  8.24 us (2%)
  other arithmetic  4.32 us (1%)
    pallas_call x1, Pallas kernels, channelize(): pl.pallas_call(functools.partial(channelize_kernel, count, slots, taps.sh...  136 us
    another operation x1, local copies, waits for them, and re-layouts, clean(): data = turned.reshape(channels, frames, parts * inputs_local)  69.1 us
    reshape x2, local copies, waits for them, and re-layouts, channelize(): turned.reshape(count, CHUNKS, 2, count * slots, rows, 2, LANES // 2)  65.9 us
    psum x1, waiting for transfers between devices, clean(): gram = jnp.transpose(lax.psum(gram, 'inp'), (1, 2, 0))  38.9 us
    unnamed x6, local copies, waits for them, and re-layouts  7.66 us
  transfers between devices with their start and end apart: 1, of which 1 were waited for; matrix products, arithmetic and copies ran while one was open for 0% of the time, Pallas kernels for 0%

profile of v1, /device:TPU:0, one launch (start us, length us, event | category | flops | bytes accessed | tf_op | source)
XLA Modules:
  0.0 359.2 jit_solution(11853877640213873064)
XLA Ops:
  7.2 0.0 all-reduce.2.cloned.1.call-start
  7.2 6.6 %copy.9 = s32[3,2048,256]{1,2,0:T(8,128)} copy(s32[3,2048,256]{2,1,0:T(8,128)} %param.4) | data formatting | bytes 12582912 | tf_op args[0]
  13.9 3.6 convert_element_type.19
  17.5 0.0 copy-start.1
  17.5 1.9 copy.16
  19.4 0.0 copy-done.1
  19.4 136.4 %channelize.1 = bf16[8,2,2,384,128]{4,3,2,1,0:T(8,128)(2,1)S(1)} custom-call(bf16[8,2,3,16,2048]{4,3,2,1,0:T(8,128)(2,1)} %bitcast.18, f32[12,2048]{1,0:T(8,128)S(1)} %copy-done.1, bf16[4,1024,1024]{2,1,0:T(8,128)(2,1)} %constant.12.clone.table_hbm), custom_call_target="tpu_custom_call" | custom-call | tf_op jit(solution)/shard_map/channelize/pallas_call | solution.py:149
  155.8 5.4 %reshape.21 = bf16[8,2,2,24,16,2,64]{6,5,4,3,2,1,0:T(2,128)(2,1)} reshape(bf16[8,2,2,384,128]{4,3,2,1,0:T(8,128)(2,1)S(1)} %channelize.1) | data formatting | bytes 6291456 | tf_op jit(solution)/shard_map/reshape | solution.py:170
  161.2 60.5 %copy.11 = bf16[8,2,2,24,16,2,64]{4,1,0,5,3,2,6:T(2,128)(2,1)} copy(bf16[8,2,2,24,16,2,64]{6,5,4,3,2,1,0:T(2,128)(2,1)} %reshape.21) | data formatting | bytes 6291456 | tf_op jit(solution)/shard_map/reshape | solution.py:170
  221.7 69.1 %reshape_reshape.3 = bf16[128,24,512]{2,1,0:T(8,128)(2,1)S(1)} reshape(bf16[64,2,24,2,8,2,16]{6,5,4,3,2,1,0:T(2,128)(2,1)} %bitcast.17) | data formatting | bytes 6291456 | tf_op jit(solution)/shard_map/reshape;reshape | solution.py:215
  290.8 0.7 fusion.4
  291.5 0.1 broadcast_in_dim.2
  291.6 2.5 fusion
  294.1 2.6 copy.12
  296.7 0.0 all-reduce.2.cloned.1.call-update
  296.7 38.9 %all-reduce.2.cloned.1.call-done.gram_ref = f32[32,24,128]{2,1,0:T(8,128)} async-done(((f32[32,24,128]{2,1,0:T(8,128)}), f32[32,24,128]{2,1,0:T(8,128)}) %all-reduce.2.cloned.1.call-update) | async-done | bytes 393232 | tf_op jit(solution)/shard_map/psum | solution.py:221
  335.6 0.0 copy-start
  335.6 1.0 copy-done
  336.6 2.9 subspace.1
  339.6 1.6 copy.13
  341.2 5.7 %convolution_convert_fusion = bf16[128,24,512]{2,1,0:T(8,128)(2,1)} fusion(f32[128,24,24]{2,1,0:T(8,128)} %copy.13, bf16[128,24,512]{2,1,0:T(8,128)(2,1)S(1)} %reshape_reshape.3), kind=kOutput, calls=%fused_computation.5 | convolution fusion | flops 454557696 | bytes 6586368 | tf_op jit(solution)/shard_map/cmn,cnr->cmr/dot_general | solution.py:232
  346.9 5.5 %reshape.22 = bf16[128,24,2,256]{3,2,1,0:T(2,128)(2,1)} reshape(bf16[128,24,512]{2,1,0:T(8,128)(2,1)} %convolution_convert_fusion) | data formatting | bytes 6291456 | tf_op jit(solution)/shard_map/reshape | solution.py:235
  (1 shorter events, 0.0 us)
Async XLA Ops:
  7.2 328.4 %all-reduce.2.cloned.1.call-start = ((), (), s32[]{:S(2)}) async-start(), calls=%async_computation | async-start | bytes 786432 | tf_op jit(solution)/shard_map/psum | solution.py:221
  17.5 1.9 copy-start.1
  335.6 1.0 copy-start
Sparse Core Ops, SparseCore 0:
  296.9 38.7 all-reduce.1

commit v2 on v1

--- a/solution.py
+++ b/solution.py
@@ -35,8 +35,8 @@
 
 
 def channelize_kernel(
-    count, slots, tap_count, volts_ref, taps_ref, table_hbm, turned_ref,
-    gathered, table, halves, outgoing, table_sem, send_a, recv_a, send_b, recv_b,
+    count, slots, tap_count, volts_ref, taps_ref, table_hbm, spectra_ref,
+    gathered, table, halves, outgoing, landed, table_sem, send_a, recv_a, send_b, recv_b,
 ):
     me = lax.axis_index("freq")
     frames = count * slots
@@ -66,7 +66,7 @@
         peer = lax.rem(me + step, count)
         return pltpu.make_async_remote_copy(
             src_ref=outgoing.at[peer, chunk],
-            dst_ref=turned_ref.at[me, chunk],
+            dst_ref=landed.at[me, chunk],
             send_sem=send_b.at[chunk, step - 1],
             recv_sem=recv_b.at[chunk, step - 1],
             device_id={"freq": peer},
@@ -130,10 +130,19 @@
         lax.fori_loop(0, count // 2, transform_tile, 0)
         for step in order:
             spectra_copy(chunk, step).start()
-        turned_ref[me, chunk] = outgoing[me, chunk]
+        landed[me, chunk] = outgoing[me, chunk]
     for chunk in range(CHUNKS):
         for step in order:
             spectra_copy(chunk, step).wait()
+
+        def turn_frame(index, carry):
+            parity, frame = lax.div(index, frames), lax.rem(index, frames)
+            at = pl.ds(pl.multiple_of(frame * rows, rows), rows)
+            block = landed[:, chunk, parity, at, :].reshape(count * rows, LANES)
+            spectra_ref[parity, frame, :, chunk * LANES : (chunk + 1) * LANES] = block.T
+            return carry
+
+        lax.fori_loop(0, 2 * frames, turn_frame, 0)
 
 
 def channelize(voltages, taps):
@@ -141,20 +150,21 @@
     count = lax.axis_size("freq")
     half = frame_len // 2
     rows = inputs_local // (count * CHUNKS)
-    volts = voltages.astype(jnp.bfloat16).reshape(slots, frame_len, count, CHUNKS, rows)
-    volts = jnp.transpose(volts, (2, 3, 0, 4, 1))
+    volts = voltages.astype(jnp.bfloat16).reshape(slots, frame_len, CHUNKS, count, rows)
+    volts = jnp.transpose(volts, (3, 2, 0, 4, 1))
     table = jnp.asarray(dft_tables(frame_len, count))
     all_rows = count * slots * rows
     vmem = pl.BlockSpec(memory_space=pltpu.VMEM)
-    turned = pl.pallas_call(
+    spectra = pl.pallas_call(
         functools.partial(channelize_kernel, count, slots, taps.shape[0]),
-        out_shape=jax.ShapeDtypeStruct((count, CHUNKS, 2, all_rows, LANES), jnp.bfloat16),
+        out_shape=jax.ShapeDtypeStruct((2, count * slots, LANES, inputs_local), jnp.bfloat16),
         in_specs=[vmem, vmem, pl.BlockSpec(memory_space=pl.ANY)],
         out_specs=vmem,
         scratch_shapes=[
             pltpu.VMEM((CHUNKS, count, slots, rows, frame_len), jnp.bfloat16),
             pltpu.VMEM((4, half, half), jnp.bfloat16),
             pltpu.VMEM((4, all_rows, half), jnp.bfloat16),
+            pltpu.VMEM((count, CHUNKS, 2, all_rows, LANES), jnp.bfloat16),
             pltpu.VMEM((count, CHUNKS, 2, all_rows, LANES), jnp.bfloat16),
             pltpu.SemaphoreType.DMA,
             pltpu.SemaphoreType.DMA((CHUNKS, count - 1)),
@@ -167,12 +177,42 @@
         ),
         name="channelize",
     )(volts, taps, table)
-    turned = turned.reshape(count, CHUNKS, 2, count * slots, rows, 2, LANES // 2)
-    turned = jnp.transpose(turned, (6, 2, 3, 5, 0, 1, 4))
-    return turned.reshape(LANES, count * slots, 2, inputs_local)
-
-
-def subspace_kernel(gram_ref, keep_ref, ritz_ref):
+    spectra = spectra.reshape(2, count * slots, 2, LANES // 2, inputs_local)
+    spectra = jnp.transpose(spectra, (3, 0, 1, 2, 4))
+    return spectra.reshape(LANES, count * slots, 2, inputs_local)
+
+
+def subspace_kernel(
+    own_ref, keep_ref, ritz_ref, gram_ref, from_core, from_chip, send_sem, recv_sem
+):
+    me = lax.axis_index("inp")
+    core = lax.rem(me, 2)
+    other_core = me + 1 - 2 * core
+    other_chip = lax.rem(me + 2, 4)
+    barrier = pltpu.get_barrier_semaphore()
+    for peer in (other_core, other_chip):
+        pl.semaphore_signal(barrier, inc=1, device_id={"inp": peer}, device_id_type=MESH)
+    pl.semaphore_wait(barrier, 2)
+    rows = from_core.shape[0]
+    mine, other = pl.ds(core * rows, rows), pl.ds((1 - core) * rows, rows)
+
+    def exchange(phase, source, target, peer):
+        copy = pltpu.make_async_remote_copy(
+            src_ref=source,
+            dst_ref=target,
+            send_sem=send_sem.at[phase],
+            recv_sem=recv_sem.at[phase],
+            device_id={"inp": peer},
+            device_id_type=MESH,
+        )
+        copy.start()
+        copy.wait()
+
+    exchange(0, own_ref.at[other], from_core, other_core)
+    gram_ref[mine] = own_ref[mine] + from_core[...]
+    exchange(1, gram_ref.at[mine], from_chip, other_chip)
+    gram_ref[mine] = gram_ref[mine] + from_chip[...]
+    exchange(2, gram_ref.at[mine], gram_ref.at[mine], other_core)
     block = ritz_ref.shape[0]
     frames = keep_ref.shape[0]
 
@@ -218,14 +258,24 @@
         [jnp.broadcast_to(begin[None], (channels,) + begin.shape), data], axis=1
     )
     gram = jnp.einsum("czr,cmr->czm", stacked, data, preferred_element_type=jnp.float32)
-    gram = jnp.transpose(lax.psum(gram, "inp"), (1, 2, 0))
+    gram = jnp.transpose(gram, (1, 2, 0))
+    half = ((block + frames) // 2, frames, channels)
     keep, ritz = pl.pallas_call(
         subspace_kernel,
         out_shape=(
             jax.ShapeDtypeStruct((frames, frames, channels), jnp.float32),
             jax.ShapeDtypeStruct((block, block, channels), jnp.float32),
         ),
-        compiler_params=pltpu.CompilerParams(vmem_limit_bytes=32 * 1024 * 1024),
+        scratch_shapes=[
+            pltpu.VMEM(gram.shape, jnp.float32),
+            pltpu.VMEM(half, jnp.float32),
+            pltpu.VMEM(half, jnp.float32),
+            pltpu.SemaphoreType.DMA((3,)),
+            pltpu.SemaphoreType.DMA((3,)),
+        ],
+        compiler_params=pltpu.CompilerParams(
+            collective_id=1, has_side_effects=True, vmem_limit_bytes=32 * 1024 * 1024
+        ),
         name="subspace",
     )(gram)
     keep = jnp.transpose(keep, (2, 0, 1))
@@ -331,8 +381,11 @@
     count = lax.axis_size("freq")
     fits = (
         count % 2 == 0
+        and lax.axis_size("inp") == 4
+        and (count * slots + start.shape[0]) % 2 == 0
         and frame_len // 2 == count * LANES
-        and inputs_local % (count * CHUNKS * 16) == 0
+        and inputs_local == CHUNKS * LANES
+        and LANES % (count * 16) == 0
         and count * slots <= 32
         and taps.shape[0] <= count * slots
     )

time: 364 us -> 194 us (0.53)
  the two profiles are of different devices: /device:TPU:0 before, /device:TPU:13 now
where the time goes in v2:
time: 194 us
  Pallas kernels  158 us (81%)
  local copies, waits for them, and re-layouts  21.3 us (11%)
  matrix products  9.09 us (5%)
  other arithmetic  4.32 us (2%)
    pallas_call x1, Pallas kernels, channelize(): pl.pallas_call(functools.partial(channelize_kernel, count, slots, taps.sh...  145 us
    pallas_call x1, Pallas kernels, clean(): pl.pallas_call(subspace_kernel, out_shape=(jax.ShapeDtypeStruct((frames,...  12.9 us
    unnamed x5, local copies, waits for them, and re-layouts  7.26 us
    dot_general x1, matrix products, clean(): jnp.einsum('cmn,cnr->cmr', keep, data.astype(jnp.float32), precision=lax....  4.99 us
    dot_general x1, matrix products, clean(): jnp.einsum('czr,cmr->czm', stacked, data, preferred_element_type=jnp.floa...  4.1 us

profile of v2, /device:TPU:13, one launch (start us, length us, event | category | flops | bytes accessed | tf_op | source)
XLA Modules:
  0.0 193.5 jit_solution(2369490142561512266)
XLA Ops:
  0.6 6.6 %copy.9 = s32[3,2048,256]{1,2,0:T(8,128)} copy(s32[3,2048,256]{2,1,0:T(8,128)} %param.4) | data formatting | bytes 12582912 | tf_op args[0]
  7.3 3.6 %convert_element_type.19 = bf16[3,2048,256]{1,2,0:T(8,128)(2,1)S(1)} convert(s32[3,2048,256]{1,2,0:T(8,128)} %copy.9) | non-fusion elementwise | flops 1572864 | bytes 9437184 | tf_op jit(solution)/shard_map/convert_element_type | solution.py:153
  10.9 0.0 copy-start
  10.9 1.9 copy.16
  12.8 0.0 copy-done
  12.8 145.2 %channelize.1 = bf16[2,24,128,256]{3,2,1,0:T(8,128)(2,1)S(1)} custom-call(bf16[8,2,3,16,2048]{4,3,2,1,0:T(8,128)(2,1)} %bitcast.20, f32[12,2048]{1,0:T(8,128)S(1)} %copy-done, bf16[4,1024,1024]{2,1,0:T(8,128)(2,1)} %constant.12.clone.table_hbm), custom_call_target="tpu_custom_call" | custom-call | tf_op jit(solution)/shard_map/channelize/pallas_call | solution.py:158
  158.0 3.2 %copy.11 = bf16[64,2,24,2,256]{4,3,2,1,0:T(2,128)(2,1)S(1)} copy(bf16[64,2,24,2,256]{4,0,3,2,1:T(8,128)(2,1)S(1)} %bitcast.16) | data formatting | bytes 6291456 | tf_op jit(solution)/shard_map/transpose | solution.py:181
  161.2 3.7 %reshape_reshape.3 = bf16[128,24,512]{2,1,0:T(8,128)(2,1)} reshape(bf16[64,2,24,2,256]{4,3,2,1,0:T(2,128)(2,1)S(1)} %copy.11) | data formatting | bytes 6291456 | tf_op jit(solution)/shard_map/reshape;reshape | solution.py:255
  165.0 0.7 fusion.4
  165.7 0.1 broadcast_in_dim.2
  165.8 4.1 %fusion = f32[128,32,24]{1,2,0:T(8,128)S(1)} fusion(bf16[128,24,512]{2,1,0:T(8,128)(2,1)} %reshape_reshape.3, bf16[128,8,512]{2,1,0:T(8,128)(2,1)S(1)} %broadcast_in_dim.2), kind=kOutput, calls=%fused_computation | convolution fusion | flops 109051904 | bytes 4587520 | tf_op jit(solution)/shard_map/czr,cmr->czm/dot_general | solution.py:260
  169.9 0.5 copy.12
  170.4 12.9 %subspace.1 = (f32[24,24,128]{2,1,0:T(8,128)S(1)}, f32[8,8,128]{2,1,0:T(8,128)S(1)}) custom-call(f32[32,24,128]{2,1,0:T(8,128)S(1)} %bitcast.17), custom_call_target="tpu_custom_call" | custom-call | tf_op jit(solution)/shard_map/subspace/pallas_call | solution.py:263
  183.3 1.6 copy.13
  185.0 5.0 %convolution_convert_fusion = bf16[128,24,512]{2,1,0:T(8,128)(2,1)S(1)} fusion(f32[128,24,24]{2,1,0:T(8,128)} %copy.13, bf16[128,24,512]{2,1,0:T(8,128)(2,1)} %reshape_reshape.3), kind=kOutput, calls=%fused_computation.5 | convolution fusion | flops 454557696 | bytes 6586368 | tf_op jit(solution)/shard_map/cmn,cnr->cmr/dot_general | solution.py:282
  190.0 2.9 %reshape.22 = bf16[128,24,2,256]{3,2,1,0:T(2,128)(2,1)} reshape(bf16[128,24,512]{2,1,0:T(8,128)(2,1)S(1)} %convolution_convert_fusion) | data formatting | bytes 6291456 | tf_op jit(solution)/shard_map/reshape | solution.py:285
  192.9 0.6 copy.18
  (1 shorter events, 0.0 us)
Async XLA Ops:
  10.9 1.9 copy-start

commit v3 on v2

--- a/solution.py
+++ b/solution.py
@@ -35,20 +35,45 @@
 
 
 def channelize_kernel(
-    count, slots, tap_count, volts_ref, taps_ref, table_hbm, spectra_ref,
-    gathered, table, halves, outgoing, landed, table_sem, send_a, recv_a, send_b, recv_b,
+    count, slots, tap_count, raw_hbm, taps_ref, table_hbm, spectra_ref,
+    raw, volts_ref, gathered, table, halves, outgoing, landed,
+    raw_sem, table_sem, send_a, recv_a, send_b, recv_b,
 ):
     me = lax.axis_index("freq")
     frames = count * slots
     half = table.shape[1]
     rows = volts_ref.shape[3]
 
+    raw_copies = [
+        pltpu.make_async_copy(
+            raw_hbm.at[:, :, chunk * LANES : (chunk + 1) * LANES], raw.at[chunk], raw_sem.at[chunk]
+        )
+        for chunk in range(CHUNKS)
+    ]
+    for copy in raw_copies:
+        copy.start()
     table_copy = pltpu.make_async_copy(table_hbm, table, table_sem)
     table_copy.start()
     barrier = pltpu.get_barrier_semaphore()
     for step in range(1, count):
         peer = lax.rem(me + step, count)
         pl.semaphore_signal(barrier, inc=1, device_id={"freq": peer}, device_id_type=MESH)
+
+    def turn_input(chunk):
+        raw_copies[chunk].wait()
+        width = 2 * LANES
+        tiles = 2 * half // width
+
+        def turn_tile(index, carry):
+            frame, tile = lax.div(index, tiles), lax.rem(index, tiles)
+            at = pl.ds(pl.multiple_of(tile * width, width), width)
+            block = raw[chunk, frame, at, :].astype(jnp.float32).astype(jnp.bfloat16)
+            volts_ref[:, chunk, frame, :, at] = block.T.reshape(count, rows, width)
+            return carry
+
+        lax.fori_loop(0, slots * tiles, turn_tile, 0)
+
+    turn_input(0)
     pl.semaphore_wait(barrier, count - 1)
 
     def voltage_copy(chunk, step):
@@ -74,23 +99,19 @@
         )
 
     order = sorted(range(1, count), key=lambda step: -min(step, count - step))
-    first = [voltage_copy(0, step) for step in order]
-    for copy in first:
-        copy.start()
+    for step in order:
+        voltage_copy(0, step).start()
+    gathered[0, me] = volts_ref[me, 0]
+    for chunk in range(1, CHUNKS):
+        turn_input(chunk)
+        gathered[chunk, me] = volts_ref[me, chunk]
     for chunk in range(CHUNKS):
-        gathered[chunk, me] = volts_ref[me, chunk]
-    arriving = first
-    for chunk in range(CHUNKS):
-        for copy in arriving:
-            copy.wait_send()
-        following = []
-        if chunk + 1 < CHUNKS:
-            following = [voltage_copy(chunk + 1, step) for step in order]
-            for copy in following:
-                copy.start()
-        for copy in arriving:
-            copy.wait_recv()
-        arriving = following
+        if chunk == 0:
+            for step in order:
+                voltage_copy(0, step).wait_send()
+                voltage_copy(1, step).start()
+        for step in order:
+            voltage_copy(chunk, step).wait_recv()
 
         def filter_tile(tile, carry):
             sums = []
@@ -129,6 +150,8 @@
 
         lax.fori_loop(0, count // 2, transform_tile, 0)
         for step in order:
+            if chunk == 0:
+                voltage_copy(1, step).wait_send()
             spectra_copy(chunk, step).start()
         landed[me, chunk] = outgoing[me, chunk]
     for chunk in range(CHUNKS):
@@ -139,7 +162,11 @@
             parity, frame = lax.div(index, frames), lax.rem(index, frames)
             at = pl.ds(pl.multiple_of(frame * rows, rows), rows)
             block = landed[:, chunk, parity, at, :].reshape(count * rows, LANES)
-            spectra_ref[parity, frame, :, chunk * LANES : (chunk + 1) * LANES] = block.T
+            block = block.T
+            for part in (0, 1):
+                spectra_ref[parity, part, frame, :, chunk * LANES : (chunk + 1) * LANES] = block[
+                    part * LANES // 2 : (part + 1) * LANES // 2
+                ]
             return carry
 
         lax.fori_loop(0, 2 * frames, turn_frame, 0)
@@ -150,22 +177,23 @@
     count = lax.axis_size("freq")
     half = frame_len // 2
     rows = inputs_local // (count * CHUNKS)
-    volts = voltages.astype(jnp.bfloat16).reshape(slots, frame_len, CHUNKS, count, rows)
-    volts = jnp.transpose(volts, (3, 2, 0, 4, 1))
     table = jnp.asarray(dft_tables(frame_len, count))
     all_rows = count * slots * rows
     vmem = pl.BlockSpec(memory_space=pltpu.VMEM)
     spectra = pl.pallas_call(
         functools.partial(channelize_kernel, count, slots, taps.shape[0]),
-        out_shape=jax.ShapeDtypeStruct((2, count * slots, LANES, inputs_local), jnp.bfloat16),
-        in_specs=[vmem, vmem, pl.BlockSpec(memory_space=pl.ANY)],
+        out_shape=jax.ShapeDtypeStruct((2, 2, count * slots, LANES // 2, inputs_local), jnp.bfloat16),
+        in_specs=[pl.BlockSpec(memory_space=pl.ANY), vmem, pl.BlockSpec(memory_space=pl.ANY)],
         out_specs=vmem,
         scratch_shapes=[
+            pltpu.VMEM((CHUNKS, slots, frame_len, LANES), voltages.dtype),
+            pltpu.VMEM((count, CHUNKS, slots, rows, frame_len), jnp.bfloat16),
             pltpu.VMEM((CHUNKS, count, slots, rows, frame_len), jnp.bfloat16),
             pltpu.VMEM((4, half, half), jnp.bfloat16),
             pltpu.VMEM((4, all_rows, half), jnp.bfloat16),
             pltpu.VMEM((count, CHUNKS, 2, all_rows, LANES), jnp.bfloat16),
             pltpu.VMEM((count, CHUNKS, 2, all_rows, LANES), jnp.bfloat16),
+            pltpu.SemaphoreType.DMA((CHUNKS,)),
             pltpu.SemaphoreType.DMA,
             pltpu.SemaphoreType.DMA((CHUNKS, count - 1)),
             pltpu.SemaphoreType.DMA((CHUNKS, count - 1)),
@@ -176,10 +204,9 @@
             collective_id=0, has_side_effects=True, vmem_limit_bytes=48 * 1024 * 1024
         ),
         name="channelize",
-    )(volts, taps, table)
-    spectra = spectra.reshape(2, count * slots, 2, LANES // 2, inputs_local)
+    )(voltages, taps, table)
     spectra = jnp.transpose(spectra, (3, 0, 1, 2, 4))
-    return spectra.reshape(LANES, count * slots, 2, inputs_local)
+    return spectra.reshape(LANES, 2, count * slots, inputs_local)
 
 
 def subspace_kernel(
@@ -250,15 +277,14 @@
 
 
 def clean(turned, start_local):
-    channels, frames, parts, inputs_local = turned.shape
+    channels, parts, frames, inputs_local = turned.shape
     block = start_local.shape[0]
-    data = turned.reshape(channels, frames, parts * inputs_local)
-    begin = start_local.reshape(block, parts * inputs_local).astype(jnp.bfloat16)
+    begin = jnp.swapaxes(start_local, 0, 1).astype(jnp.bfloat16)
     stacked = jnp.concatenate(
-        [jnp.broadcast_to(begin[None], (channels,) + begin.shape), data], axis=1
-    )
-    gram = jnp.einsum("czr,cmr->czm", stacked, data, preferred_element_type=jnp.float32)
-    gram = jnp.transpose(gram, (1, 2, 0))
+        [jnp.broadcast_to(begin[None], (channels,) + begin.shape), turned], axis=2
+    )
+    gram = jnp.einsum("cqzi,cqmi->cqzm", stacked, turned, preferred_element_type=jnp.float32)
+    gram = jnp.transpose(jnp.sum(gram, axis=1), (1, 2, 0))
     half = ((block + frames) // 2, frames, channels)
     keep, ritz = pl.pallas_call(
         subspace_kernel,
@@ -279,10 +305,11 @@
         name="subspace",
     )(gram)
     keep = jnp.transpose(keep, (2, 0, 1))
+    keep = jnp.broadcast_to(keep[:, None], (channels, parts, frames, frames))
     cleaned = jnp.einsum(
-        "cmn,cnr->cmr", keep, data.astype(jnp.float32), precision=lax.Precision.HIGHEST
-    )
-    cleaned = cleaned.astype(jnp.bfloat16).reshape(turned.shape)
+        "cqmn,cqni->cqmi", keep, turned.astype(jnp.float32), precision=lax.Precision.HIGHEST
+    )
+    cleaned = jnp.swapaxes(cleaned.astype(jnp.bfloat16), 1, 2)
     return cleaned, jnp.transpose(ritz, (2, 0, 1))
 
 

time: 194 us -> 176 us (0.907)
  local copies, waits for them, and re-layouts: 21.3 us -> 10.3 us
  other arithmetic: 4.32 us -> 0.73 us
  matrix products: 9.09 us -> 5.92 us
    reshape x2 -> x0, local copies, waits for them, and re-layouts: 4.83 us -> none  [the longest x1 2.94 us: clean(): cleaned = cleaned.astype(jnp.bfloat16).reshape(turned.shape)]
    another operation x1 -> x0, local copies, waits for them, and re-layouts: 3.74 us -> none  [clean(): data = turned.reshape(channels, frames, parts * inputs_local)]
    dot_general x2, matrix products: 9.09 us -> 5.92 us  [the longest x1 4.53 us: clean(): jnp.einsum('cqmn,cqni->cqmi', keep, turned.astype(jnp.float32), precision...]
    convert_element_type x1, other arithmetic: 3.59 us -> 0.73 us  [clean(): begin = jnp.swapaxes(start_local, 0, 1).astype(jnp.bfloat16)]
    unnamed x5 -> x6, local copies, waits for them, and re-layouts: 7.26 us -> 7.38 us
where the time goes in v3:
time: 176 us; the launch traced here: 175 us
  Pallas kernels  158 us (90%)
  local copies, waits for them, and re-layouts  10.3 us (6%)
  matrix products  5.92 us (3%)
    pallas_call x1, Pallas kernels, channelize(): pl.pallas_call(functools.partial(channelize_kernel, count, slots, taps.sh...  145 us
    pallas_call x1, Pallas kernels, clean(): pl.pallas_call(subspace_kernel, out_shape=(jax.ShapeDtypeStruct((frames,...  13.3 us
    unnamed x6, local copies, waits for them, and re-layouts  7.38 us
    dot_general x1, matrix products, clean(): jnp.einsum('cqmn,cqni->cqmi', keep, turned.astype(jnp.float32), precision...  4.53 us

profile of v3, /device:TPU:13, one launch (start us, length us, event | category | flops | bytes accessed | tf_op | source)
XLA Modules:
  0.0 175.5 jit_solution(6656521911814353729)
XLA Ops:
  0.6 0.7 fusion.8
  1.4 0.1 broadcast_in_dim.4
  1.4 0.0 copy-start
  1.5 0.9 copy-done
  2.4 144.6 %channelize.1 = bf16[2,2,24,64,256]{4,3,2,1,0:T(8,128)(2,1)S(1)} custom-call(s32[3,2048,256]{2,1,0:T(8,128)} %raw_hbm.1, f32[12,2048]{1,0:T(8,128)S(1)} %copy-done, bf16[4,1024,1024]{2,1,0:T(8,128)(2,1)} %constant.4.clone.table_hbm), custom_call_target="tpu_custom_call" | custom-call | tf_op jit(solution)/shard_map/channelize/pallas_call | solution.py:183
  147.0 1.8 %copy.11 = bf16[64,2,2,24,256]{4,3,2,1,0:T(8,128)(2,1)S(1)} copy(bf16[64,2,2,24,256]{4,0,3,2,1:T(8,128)(2,1)S(1)} %bitcast.14) | data formatting | bytes 6291456 | tf_op jit(solution)/shard_map/transpose | solution.py:208
  148.7 0.0 copy-start.1
  148.8 1.7 copy-done.1
  150.4 1.4 fusion.5
  151.8 0.5 copy.12
  152.3 13.3 %subspace.1 = (f32[24,24,128]{2,1,0:T(8,128)S(1)}, f32[8,8,128]{2,1,0:T(8,128)S(1)}) custom-call(f32[32,24,128]{2,1,0:T(8,128)S(1)} %bitcast.15), custom_call_target="tpu_custom_call" | custom-call | tf_op jit(solution)/shard_map/subspace/pallas_call | solution.py:289
  165.6 0.5 copy.13
  166.1 4.5 %convert_bitcast_fusion = bf16[128,24,2,256]{3,1,2,0:T(8,128)(2,1)S(1)} fusion(bf16[128,2,24,256]{3,2,1,0:T(8,128)(2,1)} %bitcast.19, f32[128,24,24]{2,1,0:T(8,128)S(1)} %copy.13), kind=kOutput, calls=%fused_computation.4 | convolution fusion | flops 454557696 | bytes 6586368 | tf_op jit(solution)/shard_map/cqmn,cqni->cqmi/dot_general | solution.py:309
  170.7 4.2 %copy.14 = bf16[128,24,2,256]{3,2,1,0:T(2,128)(2,1)} copy(bf16[128,24,2,256]{3,1,2,0:T(8,128)(2,1)S(1)} %convert_bitcast_fusion) | data formatting | bytes 6291456
  174.9 0.6 copy.17
  (1 shorter events, 0.0 us)
Async XLA Ops:
  1.4 0.9 copy-start
  148.7 1.7 copy-start.1

commit v4 on v3

--- a/solution.py
+++ b/solution.py
@@ -50,68 +50,70 @@
         )
         for chunk in range(CHUNKS)
     ]
-    for copy in raw_copies:
-        copy.start()
+    raw_copies[0].start()
     table_copy = pltpu.make_async_copy(table_hbm, table, table_sem)
-    table_copy.start()
     barrier = pltpu.get_barrier_semaphore()
     for step in range(1, count):
         peer = lax.rem(me + step, count)
         pl.semaphore_signal(barrier, inc=1, device_id={"freq": peer}, device_id_type=MESH)
 
-    def turn_input(chunk):
-        raw_copies[chunk].wait()
+    def turn_input(chunk, frame):
         width = 2 * LANES
-        tiles = 2 * half // width
-
-        def turn_tile(index, carry):
-            frame, tile = lax.div(index, tiles), lax.rem(index, tiles)
+
+        def turn_tile(tile, carry):
             at = pl.ds(pl.multiple_of(tile * width, width), width)
             block = raw[chunk, frame, at, :].astype(jnp.float32).astype(jnp.bfloat16)
             volts_ref[:, chunk, frame, :, at] = block.T.reshape(count, rows, width)
             return carry
 
-        lax.fori_loop(0, slots * tiles, turn_tile, 0)
-
-    turn_input(0)
-    pl.semaphore_wait(barrier, count - 1)
-
-    def voltage_copy(chunk, step):
+        lax.fori_loop(0, 2 * half // width, turn_tile, 0)
+
+    def voltage_copy(chunk, step, frame):
         peer = lax.rem(me + step, count)
         return pltpu.make_async_remote_copy(
-            src_ref=volts_ref.at[peer, chunk],
-            dst_ref=gathered.at[chunk, me],
-            send_sem=send_a.at[chunk, step - 1],
-            recv_sem=recv_a.at[chunk, step - 1],
+            src_ref=volts_ref.at[peer, chunk, frame],
+            dst_ref=gathered.at[chunk, me, frame],
+            send_sem=send_a.at[chunk, frame, step - 1],
+            recv_sem=recv_a.at[chunk, frame, step - 1],
             device_id={"freq": peer},
             device_id_type=MESH,
         )
 
-    def spectra_copy(chunk, step):
+    def spectra_copy(chunk, step, parity):
         peer = lax.rem(me + step, count)
         return pltpu.make_async_remote_copy(
-            src_ref=outgoing.at[peer, chunk],
-            dst_ref=landed.at[me, chunk],
-            send_sem=send_b.at[chunk, step - 1],
-            recv_sem=recv_b.at[chunk, step - 1],
+            src_ref=outgoing.at[peer, chunk, parity],
+            dst_ref=landed.at[me, chunk, parity],
+            send_sem=send_b.at[chunk, parity, step - 1],
+            recv_sem=recv_b.at[chunk, parity, step - 1],
             device_id={"freq": peer},
             device_id_type=MESH,
         )
 
     order = sorted(range(1, count), key=lambda step: -min(step, count - step))
-    for step in order:
-        voltage_copy(0, step).start()
-    gathered[0, me] = volts_ref[me, 0]
-    for chunk in range(1, CHUNKS):
-        turn_input(chunk)
+    raw_copies[0].wait()
+    raw_copies[1].start()
+    table_copy.start()
+    for frame in range(slots):
+        turn_input(0, frame)
+        if frame == 0:
+            pl.semaphore_wait(barrier, count - 1)
+        for step in order:
+            voltage_copy(0, step, frame).start()
+    raw_copies[1].wait()
+    for frame in range(slots):
+        turn_input(1, frame)
+    for chunk in range(CHUNKS):
         gathered[chunk, me] = volts_ref[me, chunk]
     for chunk in range(CHUNKS):
         if chunk == 0:
+            for frame in range(slots):
+                for step in order:
+                    voltage_copy(0, step, frame).wait_send()
+                    voltage_copy(1, step, frame).start()
+        for frame in range(slots):
             for step in order:
-                voltage_copy(0, step).wait_send()
-                voltage_copy(1, step).start()
-        for step in order:
-            voltage_copy(chunk, step).wait_recv()
+                voltage_copy(chunk, step, frame).wait_recv()
 
         def filter_tile(tile, carry):
             sums = []
@@ -150,26 +152,27 @@
 
         lax.fori_loop(0, count // 2, transform_tile, 0)
         for step in order:
-            if chunk == 0:
-                voltage_copy(1, step).wait_send()
-            spectra_copy(chunk, step).start()
+            for frame in range(slots if chunk == 0 else 0):
+                voltage_copy(1, step, frame).wait_send()
+            spectra_copy(chunk, step, 0).start()
+        for step in order:
+            spectra_copy(chunk, step, 1).start()
         landed[me, chunk] = outgoing[me, chunk]
     for chunk in range(CHUNKS):
-        for step in order:
-            spectra_copy(chunk, step).wait()
-
-        def turn_frame(index, carry):
-            parity, frame = lax.div(index, frames), lax.rem(index, frames)
-            at = pl.ds(pl.multiple_of(frame * rows, rows), rows)
-            block = landed[:, chunk, parity, at, :].reshape(count * rows, LANES)
-            block = block.T
-            for part in (0, 1):
-                spectra_ref[parity, part, frame, :, chunk * LANES : (chunk + 1) * LANES] = block[
-                    part * LANES // 2 : (part + 1) * LANES // 2
-                ]
-            return carry
-
-        lax.fori_loop(0, 2 * frames, turn_frame, 0)
+        for parity in (0, 1):
+            for step in order:
+                spectra_copy(chunk, step, parity).wait()
+
+            def turn_frame(frame, carry):
+                at = pl.ds(pl.multiple_of(frame * rows, rows), rows)
+                block = landed[:, chunk, parity, at, :].reshape(count * rows, LANES).T
+                for part in (0, 1):
+                    spectra_ref[
+                        parity, part, frame, :, chunk * LANES : (chunk + 1) * LANES
+                    ] = block[part * LANES // 2 : (part + 1) * LANES // 2]
+                return carry
+
+            lax.fori_loop(0, frames, turn_frame, 0)
 
 
 def channelize(voltages, taps):
@@ -195,10 +198,10 @@
             pltpu.VMEM((count, CHUNKS, 2, all_rows, LANES), jnp.bfloat16),
             pltpu.SemaphoreType.DMA((CHUNKS,)),
             pltpu.SemaphoreType.DMA,
-            pltpu.SemaphoreType.DMA((CHUNKS, count - 1)),
-            pltpu.SemaphoreType.DMA((CHUNKS, count - 1)),
-            pltpu.SemaphoreType.DMA((CHUNKS, count - 1)),
-            pltpu.SemaphoreType.DMA((CHUNKS, count - 1)),
+            pltpu.SemaphoreType.DMA((CHUNKS, slots, count - 1)),
+            pltpu.SemaphoreType.DMA((CHUNKS, slots, count - 1)),
+            pltpu.SemaphoreType.DMA((CHUNKS, 2, count - 1)),
+            pltpu.SemaphoreType.DMA((CHUNKS, 2, count - 1)),
         ],
         compiler_params=pltpu.CompilerParams(
             collective_id=0, has_side_effects=True, vmem_limit_bytes=48 * 1024 * 1024
@@ -268,12 +271,15 @@
         projected = times_gram(coefficients)
     for k in range(block):
         ritz_ref[k] = jnp.sum(projected * projected[k][None], axis=1) * (1.0 / frames)
-    row = lax.broadcasted_iota(jnp.int32, keep_ref.shape[1:], 0)
+    row = lax.broadcasted_iota(jnp.int32, projected.shape[1:], 0)
     for frame in range(frames):
         removed = projected[0][frame : frame + 1] * coefficients[0]
         for k in range(1, block):
             removed = removed + projected[k][frame : frame + 1] * coefficients[k]
-        keep_ref[frame] = jnp.where(row == frame, 1.0, 0.0) - removed
+        keep = jnp.where(row == frame, 1.0, 0.0) - removed
+        high = keep.astype(jnp.bfloat16).astype(jnp.float32)
+        keep_ref[frame, :frames] = high
+        keep_ref[frame, frames:] = keep - high
 
 
 def clean(turned, start_local):
@@ -289,7 +295,7 @@
     keep, ritz = pl.pallas_call(
         subspace_kernel,
         out_shape=(
-            jax.ShapeDtypeStruct((frames, frames, channels), jnp.float32),
+            jax.ShapeDtypeStruct((frames, 2 * frames, channels), jnp.float32),
             jax.ShapeDtypeStruct((block, block, channels), jnp.float32),
         ),
         scratch_shapes=[
@@ -304,11 +310,10 @@
         ),
         name="subspace",
     )(gram)
-    keep = jnp.transpose(keep, (2, 0, 1))
-    keep = jnp.broadcast_to(keep[:, None], (channels, parts, frames, frames))
-    cleaned = jnp.einsum(
-        "cqmn,cqni->cqmi", keep, turned.astype(jnp.float32), precision=lax.Precision.HIGHEST
-    )
+    keep = jnp.transpose(keep, (2, 0, 1)).astype(jnp.bfloat16)
+    keep = jnp.broadcast_to(keep[:, None], (channels, parts, frames, 2 * frames))
+    twice = jnp.concatenate([turned, turned], axis=2)
+    cleaned = jnp.einsum("cqmn,cqni->cqmi", keep, twice, preferred_element_type=jnp.float32)
     cleaned = jnp.swapaxes(cleaned.astype(jnp.bfloat16), 1, 2)
     return cleaned, jnp.transpose(ritz, (2, 0, 1))
 

time: 176 us -> 175 us (level)
  Pallas kernels: 158 us -> 156 us
    pallas_call x1, Pallas kernels: 145 us -> 142 us  [channelize(): pl.pallas_call(functools.partial(channelize_kernel, count, slots, taps.sh...]
where the time goes in v4:
time: 175 us; the launch traced here: 174 us
  Pallas kernels  156 us (89%)
  local copies, waits for them, and re-layouts  10.7 us (6%)
  matrix products  6.38 us (4%)
    pallas_call x1, Pallas kernels, channelize(): pl.pallas_call(functools.partial(channelize_kernel, count, slots, taps.sh...  142 us
    pallas_call x1, Pallas kernels, clean(): pl.pallas_call(subspace_kernel, out_shape=(jax.ShapeDtypeStruct((frames,...  13.4 us
    unnamed x6, local copies, waits for them, and re-layouts  6.52 us
    dot_general x1, matrix products, clean(): jnp.einsum('cqmn,cqni->cqmi', keep, twice, preferred_element_type=jnp.flo...  3.87 us

profile of v4, /device:TPU:13, one launch (start us, length us, event | category | flops | bytes accessed | tf_op | source)
XLA Modules:
  0.0 174.3 jit_solution(15572943364648890089)
XLA Ops:
  0.6 0.0 copy-start
  0.6 0.9 copy-done
  1.5 142.4 %channelize.1 = bf16[2,2,24,64,256]{4,3,2,1,0:T(8,128)(2,1)S(1)} custom-call(s32[3,2048,256]{2,1,0:T(8,128)} %raw_hbm.1, f32[12,2048]{1,0:T(8,128)S(1)} %copy-done, bf16[4,1024,1024]{2,1,0:T(8,128)(2,1)} %constant.4.clone.table_hbm), custom_call_target="tpu_custom_call" | custom-call | tf_op jit(solution)/shard_map/channelize/pallas_call | solution.py:186
  143.9 1.8 %copy.11 = bf16[64,2,2,24,256]{4,3,2,1,0:T(8,128)(2,1)S(1)} copy(bf16[64,2,2,24,256]{4,0,3,2,1:T(8,128)(2,1)S(1)} %bitcast.14) | data formatting | bytes 6291456 | tf_op jit(solution)/shard_map/transpose | solution.py:211
  145.7 0.0 copy-start.1
  145.7 0.8 fusion.14
  146.5 0.1 broadcast_in_dim.4
  146.6 0.8 copy-done.1
  147.4 2.5 %fusion.10 = f32[128,32,24]{1,2,0:T(8,128)} fusion(bf16[128,2,24,256]{3,2,1,0:T(8,128)(2,1)S(1)} %bitcast.17, bf16[128,2,8,256]{3,2,1,0:T(8,128)(2,1)S(1)} %broadcast_in_dim.4), kind=kOutput, calls=%fused_computation.9 | convolution fusion | flops 109051904 | bytes 4587520 | tf_op jit(solution)/shard_map/cqzi,cqmi->cqzm/dot_general | solution.py:292
  149.9 1.9 %copy.12 = f32[128,32,24]{0,2,1:T(8,128)S(1)} copy(f32[128,32,24]{1,2,0:T(8,128)} %fusion.10) | data formatting | bytes 786432 | tf_op jit(solution)/shard_map/cqzi,cqmi->cqzm/dot_general | solution.py:292
  151.8 13.4 %subspace.1 = (f32[24,48,128]{2,1,0:T(8,128)S(1)}, f32[8,8,128]{2,1,0:T(8,128)S(1)}) custom-call(f32[32,24,128]{2,1,0:T(8,128)S(1)} %bitcast.15), custom_call_target="tpu_custom_call" | custom-call | tf_op jit(solution)/shard_map/subspace/pallas_call | solution.py:295
  165.2 0.4 copy.13
  165.6 3.9 %convert_bitcast_fusion = bf16[128,24,2,256]{3,1,2,0:T(8,128)(2,1)S(1)} fusion(bf16[128,2,24,256]{3,2,1,0:T(8,128)(2,1)} %bitcast.18, bf16[128,24,48]{2,1,0:T(8,128)(2,1)S(1)} %copy.13), kind=kOutput, calls=%fused_computation.8 | convolution fusion | flops 165150720 | bytes 6586368 | tf_op jit(solution)/shard_map/cqmn,cqni->cqmi/dot_general | solution.py:316
  169.5 4.2 %copy.14 = bf16[128,24,2,256]{3,2,1,0:T(2,128)(2,1)} copy(bf16[128,24,2,256]{3,1,2,0:T(8,128)(2,1)S(1)} %convert_bitcast_fusion) | data formatting | bytes 6291456
  173.7 0.6 copy.17
  (2 shorter events, 0.0 us)
Async XLA Ops:
  0.6 0.9 copy-start
  145.7 1.7 copy-start.1

commit v5 on v4

--- a/solution.py
+++ b/solution.py
@@ -276,10 +276,7 @@
         removed = projected[0][frame : frame + 1] * coefficients[0]
         for k in range(1, block):
             removed = removed + projected[k][frame : frame + 1] * coefficients[k]
-        keep = jnp.where(row == frame, 1.0, 0.0) - removed
-        high = keep.astype(jnp.bfloat16).astype(jnp.float32)
-        keep_ref[frame, :frames] = high
-        keep_ref[frame, frames:] = keep - high
+        keep_ref[frame] = jnp.where(row == frame, 1.0, 0.0) - removed
 
 
 def clean(turned, start_local):
@@ -295,7 +292,7 @@
     keep, ritz = pl.pallas_call(
         subspace_kernel,
         out_shape=(
-            jax.ShapeDtypeStruct((frames, 2 * frames, channels), jnp.float32),
+            jax.ShapeDtypeStruct((frames, frames, channels), jnp.float32),
             jax.ShapeDtypeStruct((block, block, channels), jnp.float32),
         ),
         scratch_shapes=[
@@ -310,10 +307,11 @@
         ),
         name="subspace",
     )(gram)
-    keep = jnp.transpose(keep, (2, 0, 1)).astype(jnp.bfloat16)
-    keep = jnp.broadcast_to(keep[:, None], (channels, parts, frames, 2 * frames))
-    twice = jnp.concatenate([turned, turned], axis=2)
-    cleaned = jnp.einsum("cqmn,cqni->cqmi", keep, twice, preferred_element_type=jnp.float32)
+    keep = jnp.transpose(keep, (2, 0, 1))
+    keep = jnp.broadcast_to(keep[:, None], (channels, parts, frames, frames))
+    cleaned = jnp.einsum(
+        "cqmn,cqni->cqmi", keep, turned.astype(jnp.float32), precision=lax.Precision.HIGHEST
+    )
     cleaned = jnp.swapaxes(cleaned.astype(jnp.bfloat16), 1, 2)
     return cleaned, jnp.transpose(ritz, (2, 0, 1))
 

time: 175 us -> 174 us (level)
  no operation moved by 1% of the time
where the time goes in v5:
time: 174 us; the launch traced here: 173 us
  Pallas kernels  156 us (90%)
  local copies, waits for them, and re-layouts  10.3 us (6%)
  matrix products  5.92 us (3%)
    pallas_call x1, Pallas kernels, channelize(): pl.pallas_call(functools.partial(channelize_kernel, count, slots, taps.sh...  142 us
    pallas_call x1, Pallas kernels, clean(): pl.pallas_call(subspace_kernel, out_shape=(jax.ShapeDtypeStruct((frames,...  13.3 us
    unnamed x6, local copies, waits for them, and re-layouts  7.38 us
    dot_general x1, matrix products, clean(): jnp.einsum('cqmn,cqni->cqmi', keep, turned.astype(jnp.float32), precision...  4.53 us

profile of v5, /device:TPU:13, one launch (start us, length us, event | category | flops | bytes accessed | tf_op | source)
XLA Modules:
  0.0 173.4 jit_solution(16380241152091100513)
XLA Ops:
  0.6 0.7 fusion.8
  1.4 0.1 broadcast_in_dim.4
  1.4 0.0 copy-start
  1.5 0.9 copy-done
  2.4 142.4 %channelize.1 = bf16[2,2,24,64,256]{4,3,2,1,0:T(8,128)(2,1)S(1)} custom-call(s32[3,2048,256]{2,1,0:T(8,128)} %raw_hbm.1, f32[12,2048]{1,0:T(8,128)S(1)} %copy-done, bf16[4,1024,1024]{2,1,0:T(8,128)(2,1)} %constant.4.clone.table_hbm), custom_call_target="tpu_custom_call" | custom-call | tf_op jit(solution)/shard_map/channelize/pallas_call | solution.py:186
  144.8 1.8 %copy.11 = bf16[64,2,2,24,256]{4,3,2,1,0:T(8,128)(2,1)S(1)} copy(bf16[64,2,2,24,256]{4,0,3,2,1:T(8,128)(2,1)S(1)} %bitcast.14) | data formatting | bytes 6291456 | tf_op jit(solution)/shard_map/transpose | solution.py:211
  146.5 0.0 copy-start.1
  146.5 1.7 copy-done.1
  148.2 1.4 fusion.5
  149.6 0.5 copy.12
  150.1 13.3 %subspace.1 = (f32[24,24,128]{2,1,0:T(8,128)S(1)}, f32[8,8,128]{2,1,0:T(8,128)S(1)}) custom-call(f32[32,24,128]{2,1,0:T(8,128)S(1)} %bitcast.15), custom_call_target="tpu_custom_call" | custom-call | tf_op jit(solution)/shard_map/subspace/pallas_call | solution.py:292
  163.5 0.5 copy.13
  164.0 4.5 %convert_bitcast_fusion = bf16[128,24,2,256]{3,1,2,0:T(8,128)(2,1)S(1)} fusion(bf16[128,2,24,256]{3,2,1,0:T(8,128)(2,1)} %bitcast.19, f32[128,24,24]{2,1,0:T(8,128)S(1)} %copy.13), kind=kOutput, calls=%fused_computation.4 | convolution fusion | flops 454557696 | bytes 6586368 | tf_op jit(solution)/shard_map/cqmn,cqni->cqmi/dot_general | solution.py:312
  168.5 4.2 %copy.14 = bf16[128,24,2,256]{3,2,1,0:T(2,128)(2,1)} copy(bf16[128,24,2,256]{3,1,2,0:T(8,128)(2,1)S(1)} %convert_bitcast_fusion) | data formatting | bytes 6291456
  172.7 0.6 copy.17
  (1 shorter events, 0.0 us)
Async XLA Ops:
  1.4 0.9 copy-start
  146.5 1.7 copy-start.1
